TPU v7x, 256 devices: a whole 4x4x8 slice. The times are simulated.
256 devices in a mesh: child: 2 (over core), row: 8 (over z), col: 16 (over x, y).
Axes of the slice: x: 4, y: 4, z: 8, core: 2. Of those that a mesh axis runs over, the one named last changes fastest.
Arguments:
- parent_slab: float32 [3072, 61440], P('col', ('child', 'row')), may hold values from -6 to 6
- panel: float32 [2, 16384, 1024], P('child', 'row'), may hold values from -0.0625 to 0.0625
- slab_panel: float32 [2, 3072, 1024], P('child', 'col'), may hold values from -0.15625 to 0.15625
- diag_inverse: float32 [2, 1024, 1024], P('child', 'col', 'row'), may hold values from -6 to 6
- tile_rows: int32 [2, 128, 128], replicated, may hold values from -1 to 3839, as said below
- tile_owner: int32 [2, 128, 1], replicated, may hold values from 0 to 15; in each aligned block of 16 rows (0 to 15, 16 to 31, ..., all dimensions but the last counted through in order) at most 2 rows name the same one
Outputs:
- slab_inverse: float32 [2, 3072, 1024], P('child', 'col', 'row')
- diag_block: float32 [2, 1024, 1024], P('child', 'col', 'row')
Inputs may be any that keep to these rules, and one draw needn't show every extreme that they name: `tile_rows`: A tile's offsets lie in the column block of its owner; -1 marks padding and fills only the end of a tile. `tile_owner`: among the 16 tiles of one device (aligned blocks of one child), no owner holds more than 2.
All inputs are finite; a program needn't handle non-finite values.
Results may differ from a plain program's by a relative error of at most 0.0001.
Values sent between devices are 32-bit elements; how exact they have to be, the bound alone decides.
No kernel may reach another device: no remote copies, remote signals or barrier semaphores. Data moves between devices by JAX's collectives and lax.ppermute only.
A program may use at most 128 MiB of HBM per device.

v0:
```python
import functools

import jax
import jax.numpy as jnp
from jax import lax
from jax.experimental import pallas as pl
from jax.experimental.pallas import tpu as pltpu
from jax.sharding import PartitionSpec as P

CAP = 2
VMEM_LIMIT = 48 << 20
CHUNKS = 5
LANES = 128
SUBLANES = 8


def split(value):
    high = value.astype(jnp.bfloat16)
    low = (value - high.astype(jnp.float32)).astype(jnp.bfloat16)
    return high, low


def dot(left, right, contract=((1,), (0,))):
    return lax.dot_general(left, right, (contract, ((), ())), preferred_element_type=jnp.float32)


def rank_of(owner, tile, first):
    own = owner[tile]

    def earlier(other, rank):
        return rank + jnp.where(owner[other] == own, 1, 0)

    return lax.fori_loop(first, tile, earlier, 0)


def device_in_group():
    return lax.axis_index("child") * lax.axis_size("row") + lax.axis_index("row")


def gather_kernel(wanted, count, visit, halves, after, owner_in, rows_in, slab_in, *refs):
    outs, has, (parts, slab, rows, owner, tiles, slots, sems) = refs[:halves], refs[halves], refs[halves + 1 :][:7]
    _, slab_rows, chunk = slab.shape
    tile_len = rows.shape[1]
    visits = has.shape[0]
    owner_copy = pltpu.make_async_copy(owner_in, owner, sems.at[CHUNKS + 1])
    owner_copy.start()
    index_copy = pltpu.make_async_copy(rows_in, rows, sems.at[CHUNKS])
    index_copy.start()
    copies = []
    for place in range(CHUNKS):
        source = slab_in.at[:, place * chunk : (place + 1) * chunk]
        copies.append(pltpu.make_async_copy(source, slab.at[place], sems.at[place]))
        copies[place].start()
    mine = device_in_group()
    owner_copy.wait()

    def block_scan(slot, found):
        begin = visit(slot, mine) * count
        first, second = jnp.int32(-1), jnp.int32(-1)
        for tile in reversed(range(count)):
            hit = owner[begin + tile] == mine
            second = jnp.where(hit, first, second)
            first = jnp.where(hit, begin + tile, first)
        tile = second if wanted else first
        tiles[found] = jnp.maximum(tile, 0)
        slots[found] = slot
        has[slot] = jnp.where(tile >= 0, 1, 0)
        return found + jnp.where(tile >= 0, 1, 0)

    found = lax.fori_loop(0, visits, block_scan, 0)
    for spare in range(2):
        tiles[found + spare] = 0
    index_copy.wait()

    if halves == 1:
        stage, out_sems = refs[-2:]

        def leave(index):
            return pltpu.make_async_copy(stage.at[index], outs[0].at[slots[index]], out_sems.at[index])

        def emit(index, value):
            stage[index] = value

            @pl.when(index < found)
            def _():
                leave(index).start()

    else:
        half = visits // halves

        def emit(index, value):
            for part, out in enumerate(outs):

                @pl.when((index < found) & (slots[index] // half == part))
                def _():
                    out[slots[index] - part * half] = value

    def arrive(place):
        copies[place].wait()
        high, low = split(slab[place])
        parts[0:slab_rows, place * chunk : (place + 1) * chunk] = high
        parts[slab_rows:, place * chunk : (place + 1) * chunk] = low

    def group(step, fresh):
        index = 3 * step
        columns = jnp.concatenate([rows[pl.ds(tiles[index + k], 1), :] for k in range(2)], axis=1)
        total = jnp.zeros((2 * slab_rows, 2 * tile_len), jnp.float32)
        lanes = rows[pl.ds(tiles[index + 2], 1), :]
        lane = jnp.broadcast_to(lanes & (LANES - 1), (SUBLANES, tile_len))
        strip = jnp.broadcast_to(lanes >> 7, (SUBLANES, tile_len))
        picked = [jnp.zeros((SUBLANES, tile_len), jnp.float32)] * (slab_rows // SUBLANES)
        for place in range(CHUNKS):
            begin = place * chunk
            if fresh:
                arrive(place)
            places = lax.broadcasted_iota(jnp.int32, (chunk, 2 * tile_len), 0) + begin
            picks = jnp.where(places == columns, 1.0, 0.0).astype(jnp.bfloat16)
            total += dot(parts[:, begin : begin + chunk], picks)
            for offset in range(0, chunk, LANES):
                inside = strip == (begin + offset) // LANES
                for band in range(slab_rows // SUBLANES):
                    values = slab[place, band * SUBLANES : (band + 1) * SUBLANES, offset : offset + LANES]
                    picked[band] = jnp.where(inside, jnp.take_along_axis(values, lane, axis=1), picked[band])
        total = total[:slab_rows] + total[slab_rows:]
        emit(index, total[:, :tile_len])
        emit(index + 1, total[:, tile_len:])
        emit(index + 2, jnp.concatenate(picked, axis=0))

    @pl.when(found > 0)
    def _():
        group(0, True)

    @pl.when(found == 0)
    def _():
        for copy in copies:
            copy.wait()

    def later(step, carry):
        group(step, False)
        return carry

    lax.fori_loop(1, (found + 2) // 3, later, 0)

    if halves == 1:

        def finish(index, carry):
            leave(index).wait()
            return carry

        lax.fori_loop(0, found, finish, 0)


def gather(wanted, count, visits, halves, visit, parent_slab, rows, owner, after):
    slab_rows, width = parent_slab.shape
    tile_len = rows.shape[1]
    smem = pl.BlockSpec(memory_space=pltpu.SMEM)
    vmem = pl.BlockSpec(memory_space=pltpu.VMEM)
    hbm = pl.BlockSpec(memory_space=pl.ANY)
    scratch = [
        pltpu.VMEM((2 * slab_rows, width), jnp.bfloat16),
        pltpu.VMEM((CHUNKS, slab_rows, width // CHUNKS), jnp.float32),
        pltpu.VMEM(rows.shape, jnp.int32),
        pltpu.SMEM(owner.shape, jnp.int32),
        pltpu.SMEM((visits + 8,), jnp.int32),
        pltpu.SMEM((visits + 8,), jnp.int32),
        pltpu.SemaphoreType.DMA((CHUNKS + 2,)),
    ]
    if halves == 1:
        scratch += [pltpu.VMEM((visits + 2, slab_rows, tile_len), jnp.float32), pltpu.SemaphoreType.DMA((visits + 2,))]
    out = jax.ShapeDtypeStruct((visits // halves, slab_rows, tile_len), jnp.float32)
    return pl.pallas_call(
        functools.partial(gather_kernel, wanted, count, visit, halves),
        out_shape=(out,) * halves + (jax.ShapeDtypeStruct((visits,), jnp.int32),),
        in_specs=[hbm, hbm, hbm, hbm],
        out_specs=(hbm if halves == 1 else vmem,) * halves + (smem,),
        scratch_shapes=scratch,
        compiler_params=pltpu.CompilerParams(vmem_limit_bytes=VMEM_LIMIT),
        cost_estimate=pl.CostEstimate(flops=visits * 4 * slab_rows * width * tile_len, bytes_accessed=8 << 20, transcendentals=0),
    )(after, owner, rows, parent_slab)


def merge_kernel(has, own, passed, *outs):
    for slot, out in enumerate(outs):

        @pl.when(has[slot] > 0)
        def _():
            out[...] = own[slot]

        @pl.when(has[slot] == 0)
        def _():
            out[...] = passed[slot]


def merge(has, own, passed):
    smem = pl.BlockSpec(memory_space=pltpu.SMEM)
    vmem = pl.BlockSpec(memory_space=pltpu.VMEM)
    slots = own.shape[0]
    return pl.pallas_call(
        merge_kernel,
        out_shape=(jax.ShapeDtypeStruct(own.shape[1:], own.dtype),) * slots,
        in_specs=[smem, vmem, vmem],
        out_specs=(vmem,) * slots,
        compiler_params=pltpu.CompilerParams(vmem_limit_bytes=VMEM_LIMIT),
    )(has, own, passed)


def triple(left, right):
    left_high, left_low = split(left)
    right_high, right_low = split(right)
    return dot(
        jnp.concatenate([left_high, left_high, left_low], axis=1),
        jnp.concatenate([right_high, right_low, right_high], axis=0),
    )


def first_kernel(count, owner, me, arrived, panel_in, total, panel, sems):
    steps, depth, _ = panel.shape
    begin = me[0] * count
    copies = [
        pltpu.make_async_copy(panel_in.at[step * depth : (step + 1) * depth, :], panel.at[step], sems.at[step])
        for step in range(steps)
    ]
    for copy in copies:
        copy.start()

    def part(tile):
        return jnp.where(rank_of(owner, tile, begin) == 0, arrived[owner[tile]], 0.0)

    for step in range(steps):
        left = jnp.concatenate([part(begin + 2 * step), part(begin + 2 * step + 1)], axis=1)
        copies[step].wait()
        term = triple(left, panel[step])
        if step == 0:
            total[...] = -term
        else:
            total[...] -= term


def first_product(arrived, panel, owner, me):
    _, slab_rows, tile_len = arrived.shape
    panel_rows, width = panel.shape
    count = panel_rows // tile_len
    smem = pl.BlockSpec(memory_space=pltpu.SMEM)
    vmem = pl.BlockSpec(memory_space=pltpu.VMEM)
    return pl.pallas_call(
        functools.partial(first_kernel, count),
        out_shape=jax.ShapeDtypeStruct((slab_rows, width), jnp.float32),
        in_specs=[smem, smem, vmem, pl.BlockSpec(memory_space=pl.ANY)],
        out_specs=vmem,
        scratch_shapes=[
            pltpu.VMEM((count // 2, 2 * tile_len, width), jnp.float32),
            pltpu.SemaphoreType.DMA((count // 2,)),
        ],
        compiler_params=pltpu.CompilerParams(vmem_limit_bytes=VMEM_LIMIT),
        cost_estimate=pl.CostEstimate(flops=6 * slab_rows * width * panel_rows, bytes_accessed=16 << 20, transcendentals=0),
    )(owner, me, arrived, panel)


def second_kernel(count, place_of, owner, first, *refs):
    *arrived, panel, out, left, held, tiles, sems = refs
    tile_len = held.shape[0] // sems.shape[0]
    mine = device_in_group()
    begin = mine * count
    width = out.shape[2]

    def copy(tile, slot):
        source = panel.at[pl.ds(pl.multiple_of((tile - begin) * tile_len, tile_len), tile_len), :]
        target = held.at[pl.ds(pl.multiple_of(slot * tile_len, tile_len), tile_len), :]
        return pltpu.make_async_copy(source, target, sems.at[slot])

    def look(tile, found):
        hit = rank_of(owner, tile, begin) == 1

        @pl.when(hit)
        def _():
            tiles[found] = tile
            copy(tile, found).start()

        return found + jnp.where(hit, 1, 0)

    found = lax.fori_loop(begin, begin + count, look, 0)

    @pl.when(lax.rem(found, 2) == 1)
    def _():
        left[:, tile_len:] = jnp.zeros_like(left[:, tile_len:])
        held[pl.ds(pl.multiple_of(found * tile_len, tile_len), tile_len), :] = jnp.zeros((tile_len, held.shape[1]), jnp.float32)

    def side(slot, begin_lane):
        tile = tiles[slot]
        place = place_of(owner[tile], mine)
        for index, ref in enumerate(arrived):

            @pl.when(place == index)
            def _():
                left[:, begin_lane : begin_lane + tile_len] = ref[...]

        copy(tile, slot).wait()

    def pair(step):
        side(2 * step, 0)

        @pl.when(2 * step + 1 < found)
        def _():
            side(2 * step + 1, tile_len)

        rows = pl.ds(pl.multiple_of(2 * step * tile_len, 2 * tile_len), 2 * tile_len)
        return triple(left[...], held[rows, :])

    @pl.when(found > 0)
    def _():
        term = pair(0)
        for block in range(out.shape[0]):
            columns = slice(block * width, (block + 1) * width)
            out[block] = first[:, columns] - term[:, columns]

    @pl.when(found == 0)
    def _():
        for block in range(out.shape[0]):
            out[block] = first[:, block * width : (block + 1) * width]

    def later(step, carry):
        @pl.when(2 * step + 1 >= found)
        def _():
            left[:, tile_len:] = jnp.zeros_like(left[:, tile_len:])

        term = pair(step)
        for block in range(out.shape[0]):
            out[block] -= term[:, block * width : (block + 1) * width]
        return carry

    lax.fori_loop(1, (found + 1) // 2, later, 0)


def second_product(first, arrived, place_of, panel, owner, me, blocks):
    slab_rows, tile_len = arrived[0].shape
    panel_rows, width = panel.shape
    count = panel_rows // tile_len
    most = count // CAP
    smem = pl.BlockSpec(memory_space=pltpu.SMEM)
    vmem = pl.BlockSpec(memory_space=pltpu.VMEM)
    return pl.pallas_call(
        functools.partial(second_kernel, count, place_of),
        out_shape=jax.ShapeDtypeStruct((blocks, slab_rows, width // blocks), jnp.float32),
        in_specs=[smem, vmem] + [vmem] * len(arrived) + [pl.BlockSpec(memory_space=pl.ANY)],
        out_specs=vmem,
        scratch_shapes=[
            pltpu.VMEM((slab_rows, 2 * tile_len), jnp.float32),
            pltpu.VMEM((most * tile_len, width), jnp.float32),
            pltpu.SMEM((most + 8,), jnp.int32),
            pltpu.SemaphoreType.DMA((most,)),
        ],
        compiler_params=pltpu.CompilerParams(vmem_limit_bytes=VMEM_LIMIT),
    )(owner, first, *arrived, panel)


def diag_kernel(terms, slab_panel, inverse, out):
    total = jnp.sum(terms[...], axis=0)
    inverse[...] = total
    right_high, right_low = split(total)
    left_high, left_low = split(slab_panel[...])
    both = ((0,), (0,))
    result = dot(left_high, right_high, both) + dot(left_high, right_low, both) + dot(left_low, right_high, both)
    out[...] = result.reshape(out.shape)


def diag_terms(terms, slab_panel, blocks):
    _, slab_rows, width = terms.shape
    rows = slab_panel.shape[1]
    vmem = pl.BlockSpec(memory_space=pltpu.VMEM)
    return pl.pallas_call(
        diag_kernel,
        out_shape=(
            jax.ShapeDtypeStruct((slab_rows, width), jnp.float32),
            jax.ShapeDtypeStruct((blocks, rows // blocks, width), jnp.float32),
        ),
        in_specs=[vmem, vmem],
        out_specs=(vmem, vmem),
        compiler_params=pltpu.CompilerParams(vmem_limit_bytes=VMEM_LIMIT),
    )(terms, slab_panel)


def local(parent_slab, panel, slab_panel, diag_inverse, tile_rows, tile_owner):
    row_count, col_count = lax.axis_size("row"), lax.axis_size("col")
    group_size = lax.axis_size("child") * row_count
    me = (lax.axis_index("child") * row_count + lax.axis_index("row")).astype(jnp.int32).reshape(1)
    owner = tile_owner.reshape(-1)
    rows = tile_rows.reshape(-1, tile_rows.shape[2])
    count = owner.shape[0] // group_size

    def by_child(slot, mine):
        row = lax.rem(mine, row_count)
        child = mine // row_count + slot // row_count
        return lax.rem(child * row_count + lax.rem(row + slot, row_count), group_size)

    first_columns, _ = gather(0, count, group_size, 1, lambda slot, mine: slot, parent_slab, rows, owner, me)
    after = lax.optimization_barrier((me, first_columns))[0]
    first_arrived = lax.all_to_all(first_columns, ("child", "row"), split_axis=0, concat_axis=0, tiled=True)
    own, other, has = gather(1, count, group_size, 2, by_child, parent_slab, rows, owner, after)
    passed = lax.ppermute(other, "child", [(0, 1), (1, 0)])
    merged = merge(has, own, passed)
    second_arrived = [merged[0]] + [None] * (row_count - 1)
    for step in sorted(range(1, row_count), key=lambda step: min(step, row_count - step)):
        route = [(row, (row + step) % row_count) for row in range(row_count)]
        second_arrived[step] = lax.ppermute(merged[step], "row", route)
    first = first_product(first_arrived, panel[0], owner, lax.optimization_barrier((me, *merged))[0])
    blocks = lax.optimization_barrier((owner, first_columns))[0].reshape(group_size, count)
    twice = jnp.sum((blocks[:, :, None] == jnp.arange(group_size)).astype(jnp.int32), axis=1) > 1
    single = ~jnp.any(twice[:, :row_count] & twice[:, row_count:])

    def merged_sends(first, *arrived):
        def place_of(own, mine):
            return lax.rem(mine - own + group_size, row_count)

        return second_product(first, arrived, place_of, panel[0], owner, me, row_count)

    def all_sends(first, *arrived):
        columns, _ = gather(1, count, group_size, 1, lambda slot, mine: slot, parent_slab, rows, owner, me)
        columns = lax.all_to_all(columns, ("child", "row"), split_axis=0, concat_axis=0, tiled=True)
        arrived = [columns[place] for place in range(group_size)]
        return second_product(first, arrived, lambda own, mine: own, panel[0], owner, me, row_count)

    partial = lax.cond(single, merged_sends, all_sends, first, *second_arrived)
    terms = lax.all_to_all(partial, "row", split_axis=0, concat_axis=0, tiled=True)
    slab_inverse, parts = diag_terms(terms, slab_panel[0], col_count)
    reduced = lax.all_to_all(parts, "col", split_axis=0, concat_axis=0, tiled=True)
    diag_block = diag_inverse[0] - jnp.sum(reduced, axis=0)
    return slab_inverse[None], diag_block[None]


def solution(mesh):
    in_specs = (
        P("col", ("child", "row")),
        P("child", "row", None),
        P("child", "col", None),
        P("child", "col", "row"),
        P(),
        P(),
    )
    out_specs = (P("child", "col", "row"), P("child", "col", "row"))
    return jax.shard_map(local, mesh=mesh, in_specs=in_specs, out_specs=out_specs, check_vma=False)
```

profile of v0, /device:TPU:8, one launch (start us, length us, event | category | flops | bytes accessed | tf_op | source)
XLA Modules:
  0.0 121.8 jit_solution(14916322304958299868)
XLA Ops:
  0.6 8.8 %shard_map.77 = (f32[16,192,128]{2,1,0:T(8,128)}, s32[16]{0:T(128)}) custom-call(s32[1]{0:T(128)} %bitcast.19.after.me, s32[256]{0:T(256)} %bitcast.48, s32[256,128]{1,0:T(8,128)} %bitcast.54, f32[192,3840]{1,0:T(8,128)} %slab_in.3), custom_call_target="tpu_custom_call" | custom-call | flops 6039797760 | bytes 8388608 | tf_op jit(solution)/shard_map/pallas_call | solution.py:171
  9.5 9.6 %all-to-all-start.1 = ((f32[16,192,128]{2,1,0:T(8,128)}), f32[16,192,128]{2,1,0:T(8,128)S(1)}, u32[]{:S(2)}, u32[]{:S(2)}) async-start(f32[16,192,128]{2,1,0:T(8,128)} %get-tuple-element.74), calls=%async_computation.1 | async-start | bytes 3145728 | tf_op jit(solution)/shard_map/all_to_all | solution.py:397
  19.1 2.9 %shard_map.78 = (f32[8,192,128]{2,1,0:T(8,128)S(1)}, f32[8,192,128]{2,1,0:T(8,128)}, s32[16]{0:T(128)S(1)}) custom-call(s32[1]{0:T(128)} %bitcast.19.after.me, s32[256]{0:T(256)S(1)} %bitcast.49, s32[256,128]{1,0:T(8,128)S(1)} %bitcast.55, f32[192,3840]{1,0:T(8,128)} %slab_in.3), custom_call_target="tpu_custom_call" | custom-call | flops 6039797760 | bytes 8388608 | tf_op jit(solution)/shard_map/pallas_call | solution.py:171
  22.0 0.5 collective-permute-start
  22.7 1.9 %collective-permute-done.passed = f32[8,192,128]{2,1,0:T(8,128)S(1)} collective-permute-done((f32[8,192,128]{2,1,0:T(8,128)}, f32[8,192,128]{2,1,0:T(8,128)S(1)}, u32[]{:S(2)}, u32[]{:S(2)}) %collective-permute-start) | collective-permute-done | bytes 786464 | tf_op jit(solution)/shard_map/ppermute | solution.py:399
  24.6 1.4 %shard_map.79 = (f32[192,128]{1,0:T(8,128)}, f32[192,128]{1,0:T(8,128)}, f32[192,128]{1,0:T(8,128)}, f32[192,128]{1,0:T(8,128)S(1)}, f32[192,128]{1,0:T(8,128)S(...) custom-call(s32[16]{0:T(128)S(1)} %get-tuple-element.77.has, ...), custom_call_target="tpu_custom_call" | custom-call | tf_op jit(solution)/shard_map/pallas_call | solution.py:198
  26.1 0.6 copy-done.1
  26.7 1.9 %collective-permute-start.1 = (f32[192,128]{1,0:T(8,128)}, f32[192,128]{1,0:T(8,128)S(1)}, u32[]{:S(2)}, u32[]{:S(2)}) collective-permute-start(f32[192,128]{1,0:T(8,128)} %get-tuple-element.81), channel_id=1, source_target_pairs={{0,16},{16,32},{32,48},{48,64},{64,80},{80,96},{96,112},{112,0},{1... | collective-permute-start | bytes 294920 | tf_op jit(solution)/shard_map/ppermute | solution.py:404
  28.6 2.4 %collective-permute-start.2 = (f32[192,128]{1,0:T(8,128)}, f32[192,128]{1,0:T(8,128)S(1)}, u32[]{:S(2)}, u32[]{:S(2)}) collective-permute-start(f32[192,128]{1,0:T(8,128)} %get-tuple-element.82), channel_id=1, source_target_pairs={{0,32},{16,48},{32,64},{48,80},{64,96},{80,112},{96,0},{112,16},{1... | collective-permute-start | bytes 294920 | tf_op jit(solution)/shard_map/ppermute | solution.py:404
  30.9 0.7 fusion
  32.3 9.8 %collective-permute-start.3 = (f32[192,128]{1,0:T(8,128)}, f32[192,128]{1,0:T(8,128)S(1)}, u32[]{:S(2)}, u32[]{:S(2)}) collective-permute-start(f32[192,128]{1,0:T(8,128)} %copy-done.1), channel_id=1, source_target_pairs={{0,48},{16,64},{32,80},{48,96},{64,112},{80,0},{96,16},{112,32},{1... | collective-permute-start | bytes 294920 | tf_op jit(solution)/shard_map/ppermute | solution.py:404
  42.1 4.6 %collective-permute-start.5 = (f32[192,128]{1,0:T(8,128)S(1)}, f32[192,128]{1,0:T(8,128)S(1)}, u32[]{:S(2)}, u32[]{:S(2)}) collective-permute-start(f32[192,128]{1,0:T(8,128)S(1)} %get-tuple-element.85), channel_id=1, source_target_pairs={{0,80},{16,96},{32,112},{48,0},{64,16},{80,32},{96,48},{112,64},{1... | collective-permute-start | bytes 294920 | tf_op jit(solution)/shard_map/ppermute | solution.py:404
  46.7 13.2 %collective-permute-done.1 = f32[192,128]{1,0:T(8,128)S(1)} collective-permute-done((f32[192,128]{1,0:T(8,128)}, f32[192,128]{1,0:T(8,128)S(1)}, u32[]{:S(2)}, u32[]{:S(2)}) %collective-permute-start.1) | collective-permute-done | bytes 98336 | tf_op jit(solution)/shard_map/ppermute | solution.py:404
  59.8 2.3 %collective-permute-start.6 = (f32[192,128]{1,0:T(8,128)S(1)}, f32[192,128]{1,0:T(8,128)S(1)}, u32[]{:S(2)}, u32[]{:S(2)}) collective-permute-start(f32[192,128]{1,0:T(8,128)S(1)} %get-tuple-element.86), channel_id=1, source_target_pairs={{0,96},{16,112},{32,0},{48,16},{64,32},{80,48},{96,64},{112,80},{1... | collective-permute-start | bytes 294920 | tf_op jit(solution)/shard_map/ppermute | solution.py:404
  62.1 1.7 %collective-permute-done.2 = f32[192,128]{1,0:T(8,128)S(1)} collective-permute-done((f32[192,128]{1,0:T(8,128)}, f32[192,128]{1,0:T(8,128)S(1)}, u32[]{:S(2)}, u32[]{:S(2)}) %collective-permute-start.2) | collective-permute-done | bytes 98336 | tf_op jit(solution)/shard_map/ppermute | solution.py:404
  63.8 2.2 %collective-permute-start.7 = (f32[192,128]{1,0:T(8,128)S(1)}, f32[192,128]{1,0:T(8,128)S(1)}, u32[]{:S(2)}, u32[]{:S(2)}) collective-permute-start(f32[192,128]{1,0:T(8,128)S(1)} %get-tuple-element.87), channel_id=1, source_target_pairs={{0,112},{16,0},{32,16},{48,32},{64,48},{80,64},{96,80},{112,96},{1... | collective-permute-start | bytes 294920 | tf_op jit(solution)/shard_map/ppermute | solution.py:404
  66.1 7.0 %shard_map.80 = f32[192,1024]{1,0:T(8,128)S(1)} custom-call(s32[256]{0:T(256)S(1)} %bitcast.51, s32[1]{0:T(128)} %bitcast.19.after.me, f32[16,192,128]{2,1,0:T(8,128)S(1)} %all-to-all-done.1.arrived, f32[2048,1024]{1,0:T(8,128)} %bitcast.43), custom_call_target="tpu_custom_call" | custom-call | flops 2415919104 | bytes 16777216 | tf_op jit(solution)/shard_map/pallas_call | solution.py:245
  73.1 3.7 %collective-permute-done.4 = f32[192,128]{1,0:T(8,128)S(1)} collective-permute-done((f32[192,128]{1,0:T(8,128)S(1)}, f32[192,128]{1,0:T(8,128)S(1)}, u32[]{:S(2)}, u32[]{:S(2)}) %collective-permute-start.4) | collective-permute-done | bytes 98336 | tf_op jit(solution)/shard_map/ppermute | solution.py:404
  76.8 3.2 %conditional.1 = (f32[8,192,128]{2,1,0:T(8,128)S(1)}) conditional(s32[]{:T(128)} %convert_element_type.7, (s32[1]{0:T(128)}, s32[256]{0:T(256)S(1)}, s32[256,128]{1,0:T(8,128)S(1)}, f32[192,3840]{1,0:T(8,128)S(1)}, f32[1,2048,1024]{2,1,0:T(8,128)}, /*index=5*/f32[192,1024]{1,0:T(8,128)S(1)}) %tuple.44, (f32[1,2048,1024]{2,1,0:T(8,128)}, ...), branch_computations={%region_2.0_spmd, %region_3.0_spmd} | conditional | flops 6039797760 | bytes 39845944 | solution.py:422
  76.8 3.2 %branch_1_fun.1 = f32[8,192,128]{2,1,0:T(8,128)S(1)} custom-call(s32[256]{0:T(256)S(1)} %get-tuple-element.44.owner, f32[192,1024]{1,0:T(8,128)S(1)} %get-tuple-element.45.first, f32[192,128]{1,0:T(8,128)S(1)} %get-tuple-element.46.refs_0_, f32[192,128]{1,0:T(8,128)S(1)} %get-tuple-element.47.refs_1_, f32[192,128]{1,0:T(8,128)S(1)} %get-tuple-element.48.refs_2_, ...), custom_call_target="tpu_custom_call" | custom-call | tf_op jit(solution)/shard_map/cond/branch_1_fun/pallas_call | solution.py:341
  80.1 24.4 %all_to_all.20.terms = f32[8,192,128]{2,1,0:T(8,128)S(1)} all-to-all(f32[8,192,128]{2,1,0:T(8,128)S(1)} %get-tuple-element.107), channel_id=1, replica_groups=mesh['child'=2,'row'=8,'col'=16] {'row'}, dimensions={0} | all-to-all | bytes 1572864 | tf_op jit(solution)/shard_map/all_to_all | solution.py:423
  104.5 0.7 shard_map.81
  105.2 15.9 %all_to_all.21 = f32[16,64,128]{2,1,0:T(8,128)S(1)} all-to-all(f32[16,64,128]{2,1,0:T(8,128)S(1)} %get-tuple-element.90), channel_id=1, replica_groups=mesh['child'=2,'row'=8,'col'=16] {'col'}, dimensions={0} | all-to-all | bytes 1048576 | tf_op jit(solution)/shard_map/all_to_all | solution.py:425
  121.1 0.6 bitcast_subtract_fusion
  (25 shorter events, 0.3 us)
Async XLA Ops:
  9.4 9.7 %copy-start.4 = (s32[2,128,1]{1,2,0:T(1,128)S(1)}, s32[2,128,1]{1,2,0:T(1,128)}, u32[]{:S(2)}) copy-start(s32[2,128,1]{1,2,0:T(1,128)} %param.13) | copy-start | bytes 3076
  9.4 9.7 %copy-start.6 = (s32[2,128,128]{2,1,0:T(8,128)S(1)}, s32[2,128,128]{2,1,0:T(8,128)}, u32[]{:S(2)}) copy-start(s32[2,128,128]{2,1,0:T(8,128)} %param.12) | copy-start | bytes 393220
  9.5 56.6 %all-to-all-start.1 = ((f32[16,192,128]{2,1,0:T(8,128)}), f32[16,192,128]{2,1,0:T(8,128)S(1)}, u32[]{:S(2)}, u32[]{:S(2)}) async-start(f32[16,192,128]{2,1,0:T(8,128)} %get-tuple-element.74), calls=%async_computation.1 | async-start | bytes 3145728 | tf_op jit(solution)/shard_map/all_to_all | solution.py:397
  22.0 2.6 %collective-permute-start = (f32[8,192,128]{2,1,0:T(8,128)}, f32[8,192,128]{2,1,0:T(8,128)S(1)}, u32[]{:S(2)}, u32[]{:S(2)}) collective-permute-start(f32[8,192,128]{2,1,0:T(8,128)} %get-tuple-element.79), channel_id=1, source_target_pairs={{0,128},{128,0},{1,129},{129,1},{2,130},{130,2},{3,131},{131,3},{4... | collective-permute-start | bytes 2359304 | tf_op jit(solution)/shard_map/ppermute | solution.py:399
  26.1 0.6 copy-start.1
  26.7 33.1 %collective-permute-start.1 = (f32[192,128]{1,0:T(8,128)}, f32[192,128]{1,0:T(8,128)S(1)}, u32[]{:S(2)}, u32[]{:S(2)}) collective-permute-start(f32[192,128]{1,0:T(8,128)} %get-tuple-element.81), channel_id=1, source_target_pairs={{0,16},{16,32},{32,48},{48,64},{64,80},{80,96},{96,112},{112,0},{1... | collective-permute-start | bytes 294920 | tf_op jit(solution)/shard_map/ppermute | solution.py:404
  28.6 35.2 %collective-permute-start.2 = (f32[192,128]{1,0:T(8,128)}, f32[192,128]{1,0:T(8,128)S(1)}, u32[]{:S(2)}, u32[]{:S(2)}) collective-permute-start(f32[192,128]{1,0:T(8,128)} %get-tuple-element.82), channel_id=1, source_target_pairs={{0,32},{16,48},{32,64},{48,80},{64,96},{80,112},{96,0},{112,16},{1... | collective-permute-start | bytes 294920 | tf_op jit(solution)/shard_map/ppermute | solution.py:404
  32.3 40.7 %collective-permute-start.3 = (f32[192,128]{1,0:T(8,128)}, f32[192,128]{1,0:T(8,128)S(1)}, u32[]{:S(2)}, u32[]{:S(2)}) collective-permute-start(f32[192,128]{1,0:T(8,128)} %copy-done.1), channel_id=1, source_target_pairs={{0,48},{16,64},{32,80},{48,96},{64,112},{80,0},{96,16},{112,32},{1... | collective-permute-start | bytes 294920 | tf_op jit(solution)/shard_map/ppermute | solution.py:404
  42.1 34.7 %collective-permute-start.4 = (f32[192,128]{1,0:T(8,128)S(1)}, f32[192,128]{1,0:T(8,128)S(1)}, u32[]{:S(2)}, u32[]{:S(2)}) collective-permute-start(f32[192,128]{1,0:T(8,128)S(1)} %get-tuple-element.84), channel_id=1, source_target_pairs={{0,64},{16,80},{32,96},{48,112},{64,0},{80,16},{96,32},{112,48},{1... | collective-permute-start | bytes 294920 | tf_op jit(solution)/shard_map/ppermute | solution.py:404
  42.1 34.7 %collective-permute-start.5 = (f32[192,128]{1,0:T(8,128)S(1)}, f32[192,128]{1,0:T(8,128)S(1)}, u32[]{:S(2)}, u32[]{:S(2)}) collective-permute-start(f32[192,128]{1,0:T(8,128)S(1)} %get-tuple-element.85), channel_id=1, source_target_pairs={{0,80},{16,96},{32,112},{48,0},{64,16},{80,32},{96,48},{112,64},{1... | collective-permute-start | bytes 294920 | tf_op jit(solution)/shard_map/ppermute | solution.py:404
  59.8 16.9 %collective-permute-start.6 = (f32[192,128]{1,0:T(8,128)S(1)}, f32[192,128]{1,0:T(8,128)S(1)}, u32[]{:S(2)}, u32[]{:S(2)}) collective-permute-start(f32[192,128]{1,0:T(8,128)S(1)} %get-tuple-element.86), channel_id=1, source_target_pairs={{0,96},{16,112},{32,0},{48,16},{64,32},{80,48},{96,64},{112,80},{1... | collective-permute-start | bytes 294920 | tf_op jit(solution)/shard_map/ppermute | solution.py:404
  63.8 13.0 %collective-permute-start.7 = (f32[192,128]{1,0:T(8,128)S(1)}, f32[192,128]{1,0:T(8,128)S(1)}, u32[]{:S(2)}, u32[]{:S(2)}) collective-permute-start(f32[192,128]{1,0:T(8,128)S(1)} %get-tuple-element.87), channel_id=1, source_target_pairs={{0,112},{16,0},{32,16},{48,32},{64,48},{80,64},{96,80},{112,96},{1... | collective-permute-start | bytes 294920 | tf_op jit(solution)/shard_map/ppermute | solution.py:404
  66.1 10.7 %copy-start.2 = (f32[192,128]{1,0:T(8,128)S(1)}, f32[192,128]{1,0:T(8,128)}, u32[]{:S(2)}) copy-start(f32[192,128]{1,0:T(8,128)} %get-tuple-element.80) | copy-start | bytes 294916
  66.1 10.7 %copy-start.5 = (f32[192,3840]{1,0:T(8,128)S(1)}, f32[192,3840]{1,0:T(8,128)}, u32[]{:S(2)}) copy-start(f32[192,3840]{1,0:T(8,128)} %slab_in.3) | copy-start | bytes 8847364
  66.1 10.8 %copy-start.7 = (s32[2,128,128]{2,1,0:T(8,128)S(1)}, s32[2,128,128]{2,1,0:T(8,128)}, u32[]{:S(2)}) copy-start(s32[2,128,128]{2,1,0:T(8,128)} %param.12) | copy-start | bytes 393220
  80.0 24.4 %copy-start = (f32[1,192,1024]{2,1,0:T(8,128)S(1)}, f32[1,192,1024]{2,1,0:T(8,128)}, u32[]{:S(2)}) copy-start(f32[1,192,1024]{2,1,0:T(8,128)} %param.10) | copy-start | bytes 2359300
  104.5 16.6 %copy-start.3 = (f32[1,64,128]{2,1,0:T(8,128)S(1)}, f32[1,64,128]{2,1,0:T(8,128)}, u32[]{:S(2)}) copy-start(f32[1,64,128]{2,1,0:T(8,128)} %param.11) | copy-start | bytes 98308
where the time goes:
time: 122 us
  blocking collectives  40.3 us (33%)
  starting transfers between devices  33.2 us (27%)
  Pallas kernels  24 us (20%)
  waiting for transfers between devices  20.5 us (17%)
  other arithmetic  1.48 us (1%)
  between operations  1.45 us (1%)
    all_to_all x1, blocking collectives, local(): lax.all_to_all(partial, 'row', split_axis=0, concat_axis=0, tiled=True)  24.4 us
    ppermute x7, starting transfers between devices, local(): second_arrived[step] = lax.ppermute(merged[step], 'row', route)  23.1 us
    ppermute x7, waiting for transfers between devices, local(): second_arrived[step] = lax.ppermute(merged[step], 'row', route)  18.6 us
    all_to_all x1, blocking collectives, local(): lax.all_to_all(parts, 'col', split_axis=0, concat_axis=0, tiled=True)  15.9 us
    pallas_call x2, Pallas kernels, gather(): pl.pallas_call(functools.partial(gather_kernel, wanted, count, visit, hal...  11.7 us
    all_to_all x1, starting transfers between devices, local(): lax.all_to_all(first_columns, ('child', 'row'), split_axis=0, concat_axis...  9.63 us
    pallas_call x1, Pallas kernels, first_product(): pl.pallas_call(functools.partial(first_kernel, count), out_shape=jax.Shap...  6.97 us
    pallas_call x1, Pallas kernels, second_product(): pl.pallas_call(functools.partial(second_kernel, count, place_of), out_sha...  3.19 us
  transfers between devices with their start and end apart: 9, of which 4 were waited for; matrix products, arithmetic and copies ran while one was open for 1% of the time, Pallas kernels for 9%

commit v1 on v0

--- a/solution.py
+++ b/solution.py
@@ -268,17 +268,17 @@
         target = held.at[pl.ds(pl.multiple_of(slot * tile_len, tile_len), tile_len), :]
         return pltpu.make_async_copy(source, target, sems.at[slot])
 
-    def look(tile, found):
-        hit = rank_of(owner, tile, begin) == 1
+    names = [owner[begin + tile] for tile in range(count)]
+    found = jnp.int32(0)
+    for tile in range(1, count):
+        hit = functools.reduce(jnp.logical_or, [names[tile] == name for name in names[:tile]])
 
         @pl.when(hit)
         def _():
-            tiles[found] = tile
-            copy(tile, found).start()
-
-        return found + jnp.where(hit, 1, 0)
-
-    found = lax.fori_loop(begin, begin + count, look, 0)
+            tiles[found] = begin + tile
+            copy(begin + tile, found).start()
+
+        found = found + jnp.where(hit, 1, 0)
 
     @pl.when(lax.rem(found, 2) == 1)
     def _():

time: 122 us -> 121 us (level)
  no operation moved by 1% of the time
where the time goes in v1:
time: 121 us
  blocking collectives  40.9 us (34%)
  starting transfers between devices  32 us (26%)
  Pallas kernels  23 us (19%)
  waiting for transfers between devices  20.8 us (17%)
  other arithmetic  1.48 us (1%)
  between operations  1.45 us (1%)
    all_to_all x1, blocking collectives, local(): lax.all_to_all(partial, 'row', split_axis=0, concat_axis=0, tiled=True)  25 us
    ppermute x7, starting transfers between devices, local(): second_arrived[step] = lax.ppermute(merged[step], 'row', route)  22.8 us
    ppermute x7, waiting for transfers between devices, local(): second_arrived[step] = lax.ppermute(merged[step], 'row', route)  18.9 us
    all_to_all x1, blocking collectives, local(): lax.all_to_all(parts, 'col', split_axis=0, concat_axis=0, tiled=True)  15.9 us
    pallas_call x2, Pallas kernels, gather(): pl.pallas_call(functools.partial(gather_kernel, wanted, count, visit, hal...  11.6 us
    all_to_all x1, starting transfers between devices, local(): lax.all_to_all(first_columns, ('child', 'row'), split_axis=0, concat_axis...  8.71 us
    pallas_call x1, Pallas kernels, first_product(): pl.pallas_call(functools.partial(first_kernel, count), out_shape=jax.Shap...  6.95 us
  transfers between devices with their start and end apart: 9, of which 4 were waited for; matrix products, arithmetic and copies ran while one was open for 1% of the time, Pallas kernels for 9%

profile of v1, /device:TPU:8, one launch (start us, length us, event | category | flops | bytes accessed | tf_op | source)
XLA Modules:
  0.0 120.5 jit_solution(9333824741291043866)
XLA Ops:
  0.6 8.7 %shard_map.77 = (f32[16,192,128]{2,1,0:T(8,128)}, s32[16]{0:T(128)}) custom-call(s32[1]{0:T(128)} %bitcast.19.after.me, s32[256]{0:T(256)} %bitcast.48, s32[256,128]{1,0:T(8,128)} %bitcast.54, f32[192,3840]{1,0:T(8,128)} %slab_in.3), custom_call_target="tpu_custom_call" | custom-call | flops 6039797760 | bytes 8388608 | tf_op jit(solution)/shard_map/pallas_call | solution.py:171
  9.4 8.7 %all-to-all-start.1 = ((f32[16,192,128]{2,1,0:T(8,128)}), f32[16,192,128]{2,1,0:T(8,128)S(1)}, u32[]{:S(2)}, u32[]{:S(2)}) async-start(f32[16,192,128]{2,1,0:T(8,128)} %get-tuple-element.74), calls=%async_computation.1 | async-start | bytes 3145728 | tf_op jit(solution)/shard_map/all_to_all | solution.py:397
  18.1 2.9 %shard_map.78 = (f32[8,192,128]{2,1,0:T(8,128)S(1)}, f32[8,192,128]{2,1,0:T(8,128)}, s32[16]{0:T(128)S(1)}) custom-call(s32[1]{0:T(128)} %bitcast.19.after.me, s32[256]{0:T(256)S(1)} %bitcast.49, s32[256,128]{1,0:T(8,128)S(1)} %bitcast.55, f32[192,3840]{1,0:T(8,128)} %slab_in.3), custom_call_target="tpu_custom_call" | custom-call | flops 6039797760 | bytes 8388608 | tf_op jit(solution)/shard_map/pallas_call | solution.py:171
  21.0 0.5 collective-permute-start
  21.7 1.9 %collective-permute-done.passed = f32[8,192,128]{2,1,0:T(8,128)S(1)} collective-permute-done((f32[8,192,128]{2,1,0:T(8,128)}, f32[8,192,128]{2,1,0:T(8,128)S(1)}, u32[]{:S(2)}, u32[]{:S(2)}) %collective-permute-start) | collective-permute-done | bytes 786464 | tf_op jit(solution)/shard_map/ppermute | solution.py:399
  23.6 1.4 %shard_map.79 = (f32[192,128]{1,0:T(8,128)}, f32[192,128]{1,0:T(8,128)}, f32[192,128]{1,0:T(8,128)}, f32[192,128]{1,0:T(8,128)S(1)}, f32[192,128]{1,0:T(8,128)S(...) custom-call(s32[16]{0:T(128)S(1)} %get-tuple-element.77.has, ...), custom_call_target="tpu_custom_call" | custom-call | tf_op jit(solution)/shard_map/pallas_call | solution.py:198
  25.0 0.6 copy-done.1
  25.7 1.9 %collective-permute-start.1 = (f32[192,128]{1,0:T(8,128)}, f32[192,128]{1,0:T(8,128)S(1)}, u32[]{:S(2)}, u32[]{:S(2)}) collective-permute-start(f32[192,128]{1,0:T(8,128)} %get-tuple-element.81), channel_id=1, source_target_pairs={{0,16},{16,32},{32,48},{48,64},{64,80},{80,96},{96,112},{112,0},{1... | collective-permute-start | bytes 294920 | tf_op jit(solution)/shard_map/ppermute | solution.py:404
  27.6 2.4 %collective-permute-start.2 = (f32[192,128]{1,0:T(8,128)}, f32[192,128]{1,0:T(8,128)S(1)}, u32[]{:S(2)}, u32[]{:S(2)}) collective-permute-start(f32[192,128]{1,0:T(8,128)} %get-tuple-element.82), channel_id=1, source_target_pairs={{0,32},{16,48},{32,64},{48,80},{64,96},{80,112},{96,0},{112,16},{1... | collective-permute-start | bytes 294920 | tf_op jit(solution)/shard_map/ppermute | solution.py:404
  29.9 0.7 fusion
  31.3 9.6 %collective-permute-start.3 = (f32[192,128]{1,0:T(8,128)}, f32[192,128]{1,0:T(8,128)S(1)}, u32[]{:S(2)}, u32[]{:S(2)}) collective-permute-start(f32[192,128]{1,0:T(8,128)} %copy-done.1), channel_id=1, source_target_pairs={{0,48},{16,64},{32,80},{48,96},{64,112},{80,0},{96,16},{112,32},{1... | collective-permute-start | bytes 294920 | tf_op jit(solution)/shard_map/ppermute | solution.py:404
  40.9 4.5 %collective-permute-start.5 = (f32[192,128]{1,0:T(8,128)S(1)}, f32[192,128]{1,0:T(8,128)S(1)}, u32[]{:S(2)}, u32[]{:S(2)}) collective-permute-start(f32[192,128]{1,0:T(8,128)S(1)} %get-tuple-element.85), channel_id=1, source_target_pairs={{0,80},{16,96},{32,112},{48,0},{64,16},{80,32},{96,48},{112,64},{1... | collective-permute-start | bytes 294920 | tf_op jit(solution)/shard_map/ppermute | solution.py:404
  45.4 13.5 %collective-permute-done.1 = f32[192,128]{1,0:T(8,128)S(1)} collective-permute-done((f32[192,128]{1,0:T(8,128)}, f32[192,128]{1,0:T(8,128)S(1)}, u32[]{:S(2)}, u32[]{:S(2)}) %collective-permute-start.1) | collective-permute-done | bytes 98336 | tf_op jit(solution)/shard_map/ppermute | solution.py:404
  58.8 2.3 %collective-permute-start.6 = (f32[192,128]{1,0:T(8,128)S(1)}, f32[192,128]{1,0:T(8,128)S(1)}, u32[]{:S(2)}, u32[]{:S(2)}) collective-permute-start(f32[192,128]{1,0:T(8,128)S(1)} %get-tuple-element.86), channel_id=1, source_target_pairs={{0,96},{16,112},{32,0},{48,16},{64,32},{80,48},{96,64},{112,80},{1... | collective-permute-start | bytes 294920 | tf_op jit(solution)/shard_map/ppermute | solution.py:404
  61.1 1.7 %collective-permute-done.2 = f32[192,128]{1,0:T(8,128)S(1)} collective-permute-done((f32[192,128]{1,0:T(8,128)}, f32[192,128]{1,0:T(8,128)S(1)}, u32[]{:S(2)}, u32[]{:S(2)}) %collective-permute-start.2) | collective-permute-done | bytes 98336 | tf_op jit(solution)/shard_map/ppermute | solution.py:404
  62.8 2.2 %collective-permute-start.7 = (f32[192,128]{1,0:T(8,128)S(1)}, f32[192,128]{1,0:T(8,128)S(1)}, u32[]{:S(2)}, u32[]{:S(2)}) collective-permute-start(f32[192,128]{1,0:T(8,128)S(1)} %get-tuple-element.87), channel_id=1, source_target_pairs={{0,112},{16,0},{32,16},{48,32},{64,48},{80,64},{96,80},{112,96},{1... | collective-permute-start | bytes 294920 | tf_op jit(solution)/shard_map/ppermute | solution.py:404
  65.1 7.0 %shard_map.80 = f32[192,1024]{1,0:T(8,128)S(1)} custom-call(s32[256]{0:T(256)S(1)} %bitcast.51, s32[1]{0:T(128)} %bitcast.19.after.me, f32[16,192,128]{2,1,0:T(8,128)S(1)} %all-to-all-done.1.arrived, f32[2048,1024]{1,0:T(8,128)} %bitcast.43), custom_call_target="tpu_custom_call" | custom-call | flops 2415919104 | bytes 16777216 | tf_op jit(solution)/shard_map/pallas_call | solution.py:245
  72.0 3.7 %collective-permute-done.4 = f32[192,128]{1,0:T(8,128)S(1)} collective-permute-done((f32[192,128]{1,0:T(8,128)S(1)}, f32[192,128]{1,0:T(8,128)S(1)}, u32[]{:S(2)}, u32[]{:S(2)}) %collective-permute-start.4) | collective-permute-done | bytes 98336 | tf_op jit(solution)/shard_map/ppermute | solution.py:404
  75.8 2.4 %conditional.1 = (f32[8,192,128]{2,1,0:T(8,128)S(1)}) conditional(s32[]{:T(128)} %convert_element_type.7, (s32[1]{0:T(128)}, s32[256]{0:T(256)S(1)}, s32[256,128]{1,0:T(8,128)S(1)}, f32[192,3840]{1,0:T(8,128)S(1)}, f32[1,2048,1024]{2,1,0:T(8,128)}, /*index=5*/f32[192,1024]{1,0:T(8,128)S(1)}) %tuple.44, (f32[1,2048,1024]{2,1,0:T(8,128)}, ...), branch_computations={%region_2.0_spmd, %region_3.0_spmd} | conditional | flops 6039797760 | bytes 39845944 | solution.py:422
  75.8 2.4 %branch_1_fun.1 = f32[8,192,128]{2,1,0:T(8,128)S(1)} custom-call(s32[256]{0:T(256)S(1)} %get-tuple-element.44.owner, f32[192,1024]{1,0:T(8,128)S(1)} %get-tuple-element.45.first, f32[192,128]{1,0:T(8,128)S(1)} %get-tuple-element.46.refs_0_, f32[192,128]{1,0:T(8,128)S(1)} %get-tuple-element.47.refs_1_, f32[192,128]{1,0:T(8,128)S(1)} %get-tuple-element.48.refs_2_, ...), custom_call_target="tpu_custom_call" | custom-call | tf_op jit(solution)/shard_map/cond/branch_1_fun/pallas_call | solution.py:341
  78.2 25.0 %all_to_all.20.terms = f32[8,192,128]{2,1,0:T(8,128)S(1)} all-to-all(f32[8,192,128]{2,1,0:T(8,128)S(1)} %get-tuple-element.107), channel_id=1, replica_groups=mesh['child'=2,'row'=8,'col'=16] {'row'}, dimensions={0} | all-to-all | bytes 1572864 | tf_op jit(solution)/shard_map/all_to_all | solution.py:423
  103.3 0.7 shard_map.81
  104.0 15.9 %all_to_all.21 = f32[16,64,128]{2,1,0:T(8,128)S(1)} all-to-all(f32[16,64,128]{2,1,0:T(8,128)S(1)} %get-tuple-element.90), channel_id=1, replica_groups=mesh['child'=2,'row'=8,'col'=16] {'col'}, dimensions={0} | all-to-all | bytes 1048576 | tf_op jit(solution)/shard_map/all_to_all | solution.py:425
  119.9 0.6 bitcast_subtract_fusion
  (25 shorter events, 0.3 us)
Async XLA Ops:
  9.3 8.7 %copy-start.4 = (s32[2,128,1]{1,2,0:T(1,128)S(1)}, s32[2,128,1]{1,2,0:T(1,128)}, u32[]{:S(2)}) copy-start(s32[2,128,1]{1,2,0:T(1,128)} %param.13) | copy-start | bytes 3076
  9.4 8.7 %copy-start.6 = (s32[2,128,128]{2,1,0:T(8,128)S(1)}, s32[2,128,128]{2,1,0:T(8,128)}, u32[]{:S(2)}) copy-start(s32[2,128,128]{2,1,0:T(8,128)} %param.12) | copy-start | bytes 393220
  9.4 55.7 %all-to-all-start.1 = ((f32[16,192,128]{2,1,0:T(8,128)}), f32[16,192,128]{2,1,0:T(8,128)S(1)}, u32[]{:S(2)}, u32[]{:S(2)}) async-start(f32[16,192,128]{2,1,0:T(8,128)} %get-tuple-element.74), calls=%async_computation.1 | async-start | bytes 3145728 | tf_op jit(solution)/shard_map/all_to_all | solution.py:397
  21.0 2.6 %collective-permute-start = (f32[8,192,128]{2,1,0:T(8,128)}, f32[8,192,128]{2,1,0:T(8,128)S(1)}, u32[]{:S(2)}, u32[]{:S(2)}) collective-permute-start(f32[8,192,128]{2,1,0:T(8,128)} %get-tuple-element.79), channel_id=1, source_target_pairs={{0,128},{128,0},{1,129},{129,1},{2,130},{130,2},{3,131},{131,3},{4... | collective-permute-start | bytes 2359304 | tf_op jit(solution)/shard_map/ppermute | solution.py:399
  25.0 0.6 copy-start.1
  25.7 33.1 %collective-permute-start.1 = (f32[192,128]{1,0:T(8,128)}, f32[192,128]{1,0:T(8,128)S(1)}, u32[]{:S(2)}, u32[]{:S(2)}) collective-permute-start(f32[192,128]{1,0:T(8,128)} %get-tuple-element.81), channel_id=1, source_target_pairs={{0,16},{16,32},{32,48},{48,64},{64,80},{80,96},{96,112},{112,0},{1... | collective-permute-start | bytes 294920 | tf_op jit(solution)/shard_map/ppermute | solution.py:404
  27.6 35.2 %collective-permute-start.2 = (f32[192,128]{1,0:T(8,128)}, f32[192,128]{1,0:T(8,128)S(1)}, u32[]{:S(2)}, u32[]{:S(2)}) collective-permute-start(f32[192,128]{1,0:T(8,128)} %get-tuple-element.82), channel_id=1, source_target_pairs={{0,32},{16,48},{32,64},{48,80},{64,96},{80,112},{96,0},{112,16},{1... | collective-permute-start | bytes 294920 | tf_op jit(solution)/shard_map/ppermute | solution.py:404
  31.3 40.7 %collective-permute-start.3 = (f32[192,128]{1,0:T(8,128)}, f32[192,128]{1,0:T(8,128)S(1)}, u32[]{:S(2)}, u32[]{:S(2)}) collective-permute-start(f32[192,128]{1,0:T(8,128)} %copy-done.1), channel_id=1, source_target_pairs={{0,48},{16,64},{32,80},{48,96},{64,112},{80,0},{96,16},{112,32},{1... | collective-permute-start | bytes 294920 | tf_op jit(solution)/shard_map/ppermute | solution.py:404
  40.9 34.9 %collective-permute-start.4 = (f32[192,128]{1,0:T(8,128)S(1)}, f32[192,128]{1,0:T(8,128)S(1)}, u32[]{:S(2)}, u32[]{:S(2)}) collective-permute-start(f32[192,128]{1,0:T(8,128)S(1)} %get-tuple-element.84), channel_id=1, source_target_pairs={{0,64},{16,80},{32,96},{48,112},{64,0},{80,16},{96,32},{112,48},{1... | collective-permute-start | bytes 294920 | tf_op jit(solution)/shard_map/ppermute | solution.py:404
  40.9 34.9 %collective-permute-start.5 = (f32[192,128]{1,0:T(8,128)S(1)}, f32[192,128]{1,0:T(8,128)S(1)}, u32[]{:S(2)}, u32[]{:S(2)}) collective-permute-start(f32[192,128]{1,0:T(8,128)S(1)} %get-tuple-element.85), channel_id=1, source_target_pairs={{0,80},{16,96},{32,112},{48,0},{64,16},{80,32},{96,48},{112,64},{1... | collective-permute-start | bytes 294920 | tf_op jit(solution)/shard_map/ppermute | solution.py:404
  58.8 16.9 %collective-permute-start.6 = (f32[192,128]{1,0:T(8,128)S(1)}, f32[192,128]{1,0:T(8,128)S(1)}, u32[]{:S(2)}, u32[]{:S(2)}) collective-permute-start(f32[192,128]{1,0:T(8,128)S(1)} %get-tuple-element.86), channel_id=1, source_target_pairs={{0,96},{16,112},{32,0},{48,16},{64,32},{80,48},{96,64},{112,80},{1... | collective-permute-start | bytes 294920 | tf_op jit(solution)/shard_map/ppermute | solution.py:404
  62.8 13.0 %collective-permute-start.7 = (f32[192,128]{1,0:T(8,128)S(1)}, f32[192,128]{1,0:T(8,128)S(1)}, u32[]{:S(2)}, u32[]{:S(2)}) collective-permute-start(f32[192,128]{1,0:T(8,128)S(1)} %get-tuple-element.87), channel_id=1, source_target_pairs={{0,112},{16,0},{32,16},{48,32},{64,48},{80,64},{96,80},{112,96},{1... | collective-permute-start | bytes 294920 | tf_op jit(solution)/shard_map/ppermute | solution.py:404
  65.0 10.7 %copy-start.2 = (f32[192,128]{1,0:T(8,128)S(1)}, f32[192,128]{1,0:T(8,128)}, u32[]{:S(2)}) copy-start(f32[192,128]{1,0:T(8,128)} %get-tuple-element.80) | copy-start | bytes 294916
  65.0 10.7 %copy-start.5 = (f32[192,3840]{1,0:T(8,128)S(1)}, f32[192,3840]{1,0:T(8,128)}, u32[]{:S(2)}) copy-start(f32[192,3840]{1,0:T(8,128)} %slab_in.3) | copy-start | bytes 8847364
  65.1 10.8 %copy-start.7 = (s32[2,128,128]{2,1,0:T(8,128)S(1)}, s32[2,128,128]{2,1,0:T(8,128)}, u32[]{:S(2)}) copy-start(s32[2,128,128]{2,1,0:T(8,128)} %param.12) | copy-start | bytes 393220
  78.2 25.0 %copy-start = (f32[1,192,1024]{2,1,0:T(8,128)S(1)}, f32[1,192,1024]{2,1,0:T(8,128)}, u32[]{:S(2)}) copy-start(f32[1,192,1024]{2,1,0:T(8,128)} %param.10) | copy-start | bytes 2359300
  103.3 16.6 %copy-start.3 = (f32[1,64,128]{2,1,0:T(8,128)S(1)}, f32[1,64,128]{2,1,0:T(8,128)}, u32[]{:S(2)}) copy-start(f32[1,64,128]{2,1,0:T(8,128)} %param.11) | copy-start | bytes 98308

commit v2 on v1

--- a/solution.py
+++ b/solution.py
@@ -262,6 +262,10 @@
     mine = device_in_group()
     begin = mine * count
     width = out.shape[2]
+    blocks = out.shape[0]
+
+    def ahead(block):
+        return lax.rem(block + blocks - lax.rem(mine, blocks), blocks)
 
     def copy(tile, slot):
         source = panel.at[pl.ds(pl.multiple_of((tile - begin) * tile_len, tile_len), tile_len), :]
@@ -311,12 +315,12 @@
         term = pair(0)
         for block in range(out.shape[0]):
             columns = slice(block * width, (block + 1) * width)
-            out[block] = first[:, columns] - term[:, columns]
+            out[ahead(block)] = first[:, columns] - term[:, columns]
 
     @pl.when(found == 0)
     def _():
         for block in range(out.shape[0]):
-            out[block] = first[:, block * width : (block + 1) * width]
+            out[ahead(block)] = first[:, block * width : (block + 1) * width]
 
     def later(step, carry):
         @pl.when(2 * step + 1 >= found)
@@ -325,7 +329,7 @@
 
         term = pair(step)
         for block in range(out.shape[0]):
-            out[block] -= term[:, block * width : (block + 1) * width]
+            out[ahead(block)] -= term[:, block * width : (block + 1) * width]
         return carry
 
     lax.fori_loop(1, (found + 1) // 2, later, 0)
@@ -353,8 +357,9 @@
     )(owner, first, *arrived, panel)
 
 
-def diag_kernel(terms, slab_panel, inverse, out):
-    total = jnp.sum(terms[...], axis=0)
+def diag_kernel(*refs):
+    *terms, slab_panel, inverse, out = refs
+    total = sum(term[...] for term in terms[1:]) + terms[0][...]
     inverse[...] = total
     right_high, right_low = split(total)
     left_high, left_low = split(slab_panel[...])
@@ -364,7 +369,7 @@
 
 
 def diag_terms(terms, slab_panel, blocks):
-    _, slab_rows, width = terms.shape
+    slab_rows, width = terms[0].shape
     rows = slab_panel.shape[1]
     vmem = pl.BlockSpec(memory_space=pltpu.VMEM)
     return pl.pallas_call(
@@ -373,10 +378,10 @@
             jax.ShapeDtypeStruct((slab_rows, width), jnp.float32),
             jax.ShapeDtypeStruct((blocks, rows // blocks, width), jnp.float32),
         ),
-        in_specs=[vmem, vmem],
+        in_specs=[vmem] * (len(terms) + 1),
         out_specs=(vmem, vmem),
         compiler_params=pltpu.CompilerParams(vmem_limit_bytes=VMEM_LIMIT),
-    )(terms, slab_panel)
+    )(*terms, slab_panel)
 
 
 def local(parent_slab, panel, slab_panel, diag_inverse, tile_rows, tile_owner):
@@ -420,7 +425,10 @@
         return second_product(first, arrived, lambda own, mine: own, panel[0], owner, me, row_count)
 
     partial = lax.cond(single, merged_sends, all_sends, first, *second_arrived)
-    terms = lax.all_to_all(partial, "row", split_axis=0, concat_axis=0, tiled=True)
+    terms = [partial[0]]
+    for step in range(1, row_count):
+        route = [(row, (row + step) % row_count) for row in range(row_count)]
+        terms.append(lax.ppermute(partial[step], "row", route))
     slab_inverse, parts = diag_terms(terms, slab_panel[0], col_count)
     reduced = lax.all_to_all(parts, "col", split_axis=0, concat_axis=0, tiled=True)
     diag_block = diag_inverse[0] - jnp.sum(reduced, axis=0)

time: 121 us -> 122 us (level)
  blocking collectives: 40.9 us -> 16.4 us
  waiting for transfers between devices: 20.8 us -> 34 us
  starting transfers between devices: 32 us -> 44.2 us
    all_to_all x1 -> x0, blocking collectives: 25 us -> none  [local(): lax.all_to_all(partial, 'row', split_axis=0, concat_axis=0, tiled=True)]
    ppermute x0 -> x7, waiting for transfers between devices: none -> 13.3 us  [local(): terms.append(lax.ppermute(partial[step], 'row', route))]
    ppermute x0 -> x7, starting transfers between devices: none -> 11.5 us  [local(): terms.append(lax.ppermute(partial[step], 'row', route))]
  transfers between devices with their start and end apart: 9 -> 16, of which waited for: 4 -> 9; matrix products, arithmetic and copies ran while one was open for 1% -> 1% of each run, Pallas kernels for 9% -> 9%
where the time goes in v2:
time: 122 us; the launch traced here: 121 us
  starting transfers between devices  44.2 us (36%)
  waiting for transfers between devices  34 us (28%)
  Pallas kernels  23.1 us (19%)
  blocking collectives  16.4 us (13%)
  other arithmetic  1.48 us (1%)
  between operations  1.46 us (1%)
    ppermute x7, starting transfers between devices, local(): second_arrived[step] = lax.ppermute(merged[step], 'row', route)  23 us
    ppermute x7, waiting for transfers between devices, local(): second_arrived[step] = lax.ppermute(merged[step], 'row', route)  18.7 us
    all_to_all x1, blocking collectives, local(): lax.all_to_all(parts, 'col', split_axis=0, concat_axis=0, tiled=True)  16.4 us
    ppermute x7, waiting for transfers between devices, local(): terms.append(lax.ppermute(partial[step], 'row', route))  13.3 us
    pallas_call x2, Pallas kernels, gather(): pl.pallas_call(functools.partial(gather_kernel, wanted, count, visit, hal...  11.6 us
    ppermute x7, starting transfers between devices, local(): terms.append(lax.ppermute(partial[step], 'row', route))  11.5 us
    all_to_all x1, starting transfers between devices, local(): lax.all_to_all(first_columns, ('child', 'row'), split_axis=0, concat_axis...  9.16 us
    pallas_call x1, Pallas kernels, first_product(): pl.pallas_call(functools.partial(first_kernel, count), out_shape=jax.Shap...  6.95 us
  transfers between devices with their start and end apart: 16, of which 9 were waited for; matrix products, arithmetic and copies ran while one was open for 1% of the time, Pallas kernels for 9%

profile of v2, /device:TPU:8, one launch (start us, length us, event | category | flops | bytes accessed | tf_op | source)
XLA Modules:
  0.0 121.4 jit_solution(10567797136028961718)
XLA Ops:
  0.6 8.7 %shard_map.77 = (f32[16,192,128]{2,1,0:T(8,128)}, s32[16]{0:T(128)}) custom-call(s32[1]{0:T(128)} %bitcast.19.after.me, s32[256]{0:T(256)} %bitcast.64, s32[256,128]{1,0:T(8,128)} %bitcast.70, f32[192,3840]{1,0:T(8,128)} %slab_in.3), custom_call_target="tpu_custom_call" | custom-call | flops 6039797760 | bytes 8388608 | tf_op jit(solution)/shard_map/pallas_call | solution.py:171
  9.4 9.2 %all-to-all-start.1 = ((f32[16,192,128]{2,1,0:T(8,128)}), f32[16,192,128]{2,1,0:T(8,128)S(1)}, u32[]{:S(2)}, u32[]{:S(2)}) async-start(f32[16,192,128]{2,1,0:T(8,128)} %get-tuple-element.74), calls=%async_computation.1 | async-start | bytes 3145728 | tf_op jit(solution)/shard_map/all_to_all | solution.py:402
  18.6 2.9 %shard_map.78 = (f32[8,192,128]{2,1,0:T(8,128)S(1)}, f32[8,192,128]{2,1,0:T(8,128)}, s32[16]{0:T(128)S(1)}) custom-call(s32[1]{0:T(128)} %bitcast.19.after.me, s32[256]{0:T(256)S(1)} %bitcast.65, s32[256,128]{1,0:T(8,128)S(1)} %bitcast.71, f32[192,3840]{1,0:T(8,128)} %slab_in.3), custom_call_target="tpu_custom_call" | custom-call | flops 6039797760 | bytes 8388608 | tf_op jit(solution)/shard_map/pallas_call | solution.py:171
  22.2 1.9 %collective-permute-done.passed = f32[8,192,128]{2,1,0:T(8,128)S(1)} collective-permute-done((f32[8,192,128]{2,1,0:T(8,128)}, f32[8,192,128]{2,1,0:T(8,128)S(1)}, u32[]{:S(2)}, u32[]{:S(2)}) %collective-permute-start) | collective-permute-done | bytes 786464 | tf_op jit(solution)/shard_map/ppermute | solution.py:404
  26.1 1.9 %collective-permute-start.1 = (f32[192,128]{1,0:T(8,128)}, f32[192,128]{1,0:T(8,128)S(1)}, u32[]{:S(2)}, u32[]{:S(2)}) collective-permute-start(f32[192,128]{1,0:T(8,128)} %get-tuple-element.81), channel_id=1, source_target_pairs={{0,16},{16,32},{32,48},{48,64},{64,80},{80,96},{96,112},{112,0},{1... | collective-permute-start | bytes 294920 | tf_op jit(solution)/shard_map/ppermute | solution.py:409
  28.0 8.0 %collective-permute-start.2 = (f32[192,128]{1,0:T(8,128)}, f32[192,128]{1,0:T(8,128)S(1)}, u32[]{:S(2)}, u32[]{:S(2)}) collective-permute-start(f32[192,128]{1,0:T(8,128)} %get-tuple-element.82), channel_id=1, source_target_pairs={{0,32},{16,48},{32,64},{48,80},{64,96},{80,112},{96,0},{112,16},{1... | collective-permute-start | bytes 294920 | tf_op jit(solution)/shard_map/ppermute | solution.py:409
  37.3 4.2 %collective-permute-start.3 = (f32[192,128]{1,0:T(8,128)}, f32[192,128]{1,0:T(8,128)S(1)}, u32[]{:S(2)}, u32[]{:S(2)}) collective-permute-start(f32[192,128]{1,0:T(8,128)} %copy-done.1), channel_id=1, source_target_pairs={{0,48},{16,64},{32,80},{48,96},{64,112},{80,0},{96,16},{112,32},{1... | collective-permute-start | bytes 294920 | tf_op jit(solution)/shard_map/ppermute | solution.py:409
  41.5 2.4 %collective-permute-start.4 = (f32[192,128]{1,0:T(8,128)S(1)}, f32[192,128]{1,0:T(8,128)S(1)}, u32[]{:S(2)}, u32[]{:S(2)}) collective-permute-start(f32[192,128]{1,0:T(8,128)S(1)} %get-tuple-element.84), channel_id=1, source_target_pairs={{0,64},{16,80},{32,96},{48,112},{64,0},{80,16},{96,32},{112,48},{1... | collective-permute-start | bytes 294920 | tf_op jit(solution)/shard_map/ppermute | solution.py:409
  43.9 2.1 %collective-permute-start.5 = (f32[192,128]{1,0:T(8,128)S(1)}, f32[192,128]{1,0:T(8,128)S(1)}, u32[]{:S(2)}, u32[]{:S(2)}) collective-permute-start(f32[192,128]{1,0:T(8,128)S(1)} %get-tuple-element.85), channel_id=1, source_target_pairs={{0,80},{16,96},{32,112},{48,0},{64,16},{80,32},{96,48},{112,64},{1... | collective-permute-start | bytes 294920 | tf_op jit(solution)/shard_map/ppermute | solution.py:409
  46.0 13.3 %collective-permute-done.1 = f32[192,128]{1,0:T(8,128)S(1)} collective-permute-done((f32[192,128]{1,0:T(8,128)}, f32[192,128]{1,0:T(8,128)S(1)}, u32[]{:S(2)}, u32[]{:S(2)}) %collective-permute-start.1) | collective-permute-done | bytes 98336 | tf_op jit(solution)/shard_map/ppermute | solution.py:409
  59.3 2.3 %collective-permute-start.6 = (f32[192,128]{1,0:T(8,128)S(1)}, f32[192,128]{1,0:T(8,128)S(1)}, u32[]{:S(2)}, u32[]{:S(2)}) collective-permute-start(f32[192,128]{1,0:T(8,128)S(1)} %get-tuple-element.86), channel_id=1, source_target_pairs={{0,96},{16,112},{32,0},{48,16},{64,32},{80,48},{96,64},{112,80},{1... | collective-permute-start | bytes 294920 | tf_op jit(solution)/shard_map/ppermute | solution.py:409
  63.3 2.2 %collective-permute-start.7 = (f32[192,128]{1,0:T(8,128)S(1)}, f32[192,128]{1,0:T(8,128)S(1)}, u32[]{:S(2)}, u32[]{:S(2)}) collective-permute-start(f32[192,128]{1,0:T(8,128)S(1)} %get-tuple-element.87), channel_id=1, source_target_pairs={{0,112},{16,0},{32,16},{48,32},{64,48},{80,64},{96,80},{112,96},{1... | collective-permute-start | bytes 294920 | tf_op jit(solution)/shard_map/ppermute | solution.py:409
  65.5 7.0 %shard_map.80 = f32[192,1024]{1,0:T(8,128)S(1)} custom-call(s32[256]{0:T(256)S(1)} %bitcast.67, s32[1]{0:T(128)} %bitcast.19.after.me, f32[16,192,128]{2,1,0:T(8,128)S(1)} %all-to-all-done.1.arrived, f32[2048,1024]{1,0:T(8,128)} %bitcast.59), custom_call_target="tpu_custom_call" | custom-call | flops 2415919104 | bytes 16777216 | tf_op jit(solution)/shard_map/pallas_call | solution.py:245
  72.5 3.7 %collective-permute-done.4 = f32[192,128]{1,0:T(8,128)S(1)} collective-permute-done((f32[192,128]{1,0:T(8,128)S(1)}, f32[192,128]{1,0:T(8,128)S(1)}, u32[]{:S(2)}, u32[]{:S(2)}) %collective-permute-start.4) | collective-permute-done | bytes 98336 | tf_op jit(solution)/shard_map/ppermute | solution.py:409
  76.3 2.5 %conditional.1 = (f32[8,192,128]{2,1,0:T(8,128)S(1)}) conditional(s32[]{:T(128)} %convert_element_type.7, (s32[1]{0:T(128)}, s32[256]{0:T(256)S(1)}, s32[256,128]{1,0:T(8,128)S(1)}, f32[192,3840]{1,0:T(8,128)S(1)}, f32[1,2048,1024]{2,1,0:T(8,128)}, /*index=5*/f32[192,1024]{1,0:T(8,128)S(1)}) %tuple.51, (f32[1,2048,1024]{2,1,0:T(8,128)}, ...), branch_computations={%region_2.0_spmd, %region_3.0_spmd} | conditional | flops 6039797760 | bytes 39845944 | solution.py:427
  76.3 2.5 %branch_1_fun.1 = f32[8,192,128]{2,1,0:T(8,128)S(1)} custom-call(s32[256]{0:T(256)S(1)} %get-tuple-element.44.owner, f32[192,1024]{1,0:T(8,128)S(1)} %get-tuple-element.45.first, f32[192,128]{1,0:T(8,128)S(1)} %get-tuple-element.46.refs_0_, f32[192,128]{1,0:T(8,128)S(1)} %get-tuple-element.47.refs_1_, f32[192,128]{1,0:T(8,128)S(1)} %get-tuple-element.48.refs_2_, ...), custom_call_target="tpu_custom_call" | custom-call | tf_op jit(solution)/shard_map/cond/branch_1_fun/pallas_call | solution.py:345
  79.4 3.3 %collective-permute-start.12 = (f32[192,128]{1,0:T(8,128)S(1)}, f32[192,128]{1,0:T(8,128)S(1)}, u32[]{:S(2)}, u32[]{:S(2)}) collective-permute-start(f32[192,128]{1,0:T(8,128)S(1)} %get-tuple-element.109), channel_id=1, source_target_pairs={{0,80},{16,96},{32,112},{48,0},{64,16},{80,32},{96,48},{112,64},{1... | collective-permute-start | bytes 294920 | tf_op jit(solution)/shard_map/ppermute | solution.py:431
  82.6 3.0 %collective-permute-start.11 = (f32[192,128]{1,0:T(8,128)S(1)}, f32[192,128]{1,0:T(8,128)S(1)}, u32[]{:S(2)}, u32[]{:S(2)}) collective-permute-start(f32[192,128]{1,0:T(8,128)S(1)} %get-tuple-element.110), channel_id=1, source_target_pairs={{0,64},{16,80},{32,96},{48,112},{64,0},{80,16},{96,32},{112,48},{1... | collective-permute-start | bytes 294920 | tf_op jit(solution)/shard_map/ppermute | solution.py:431
  86.0 2.2 %collective-permute-done.14.refs_7_ = f32[192,128]{1,0:T(8,128)S(1)} collective-permute-done((f32[192,128]{1,0:T(8,128)S(1)}, f32[192,128]{1,0:T(8,128)S(1)}, u32[]{:S(2)}, u32[]{:S(2)}) %collective-permute-start.14) | collective-permute-done | bytes 98336 | tf_op jit(solution)/shard_map/ppermute | solution.py:431
  90.0 2.6 %collective-permute-start.8 = (f32[192,128]{1,0:T(8,128)S(1)}, f32[192,128]{1,0:T(8,128)S(1)}, u32[]{:S(2)}, u32[]{:S(2)}) collective-permute-start(f32[192,128]{1,0:T(8,128)S(1)} %get-tuple-element.113), channel_id=1, source_target_pairs={{0,16},{16,32},{32,48},{48,64},{64,80},{80,96},{96,112},{112,0},{1... | collective-permute-start | bytes 294920 | tf_op jit(solution)/shard_map/ppermute | solution.py:431
  92.5 2.6 %collective-permute-done.11.refs_4_ = f32[192,128]{1,0:T(8,128)S(1)} collective-permute-done((f32[192,128]{1,0:T(8,128)S(1)}, f32[192,128]{1,0:T(8,128)S(1)}, u32[]{:S(2)}, u32[]{:S(2)}) %collective-permute-start.11) | collective-permute-done | bytes 98336 | tf_op jit(solution)/shard_map/ppermute | solution.py:431
  95.2 3.7 %collective-permute-done.10.refs_3_ = f32[192,128]{1,0:T(8,128)S(1)} collective-permute-done((f32[192,128]{1,0:T(8,128)S(1)}, f32[192,128]{1,0:T(8,128)S(1)}, u32[]{:S(2)}, u32[]{:S(2)}) %collective-permute-start.10) | collective-permute-done | bytes 98336 | tf_op jit(solution)/shard_map/ppermute | solution.py:431
  98.8 3.7 %collective-permute-done.9.refs_2_ = f32[192,128]{1,0:T(8,128)S(1)} collective-permute-done((f32[192,128]{1,0:T(8,128)S(1)}, f32[192,128]{1,0:T(8,128)S(1)}, u32[]{:S(2)}, u32[]{:S(2)}) %collective-permute-start.9) | collective-permute-done | bytes 98336 | tf_op jit(solution)/shard_map/ppermute | solution.py:431
  104.3 16.4 %all_to_all.15 = f32[16,64,128]{2,1,0:T(8,128)S(1)} all-to-all(f32[16,64,128]{2,1,0:T(8,128)S(1)} %get-tuple-element.90), channel_id=1, replica_groups=mesh['child'=2,'row'=8,'col'=16] {'col'}, dimensions={0} | all-to-all | bytes 1048576 | tf_op jit(solution)/shard_map/all_to_all | solution.py:433
  (39 shorter events, 10.4 us)
Async XLA Ops:
  9.4 9.2 %copy-start.4 = (s32[2,128,1]{1,2,0:T(1,128)S(1)}, s32[2,128,1]{1,2,0:T(1,128)}, u32[]{:S(2)}) copy-start(s32[2,128,1]{1,2,0:T(1,128)} %param.13) | copy-start | bytes 3076
  9.4 9.2 %copy-start.6 = (s32[2,128,128]{2,1,0:T(8,128)S(1)}, s32[2,128,128]{2,1,0:T(8,128)}, u32[]{:S(2)}) copy-start(s32[2,128,128]{2,1,0:T(8,128)} %param.12) | copy-start | bytes 393220
  9.4 56.1 %all-to-all-start.1 = ((f32[16,192,128]{2,1,0:T(8,128)}), f32[16,192,128]{2,1,0:T(8,128)S(1)}, u32[]{:S(2)}, u32[]{:S(2)}) async-start(f32[16,192,128]{2,1,0:T(8,128)} %get-tuple-element.74), calls=%async_computation.1 | async-start | bytes 3145728 | tf_op jit(solution)/shard_map/all_to_all | solution.py:402
  21.5 2.6 %collective-permute-start = (f32[8,192,128]{2,1,0:T(8,128)}, f32[8,192,128]{2,1,0:T(8,128)S(1)}, u32[]{:S(2)}, u32[]{:S(2)}) collective-permute-start(f32[8,192,128]{2,1,0:T(8,128)} %get-tuple-element.79), channel_id=1, source_target_pairs={{0,128},{128,0},{1,129},{129,1},{2,130},{130,2},{3,131},{131,3},{4... | collective-permute-start | bytes 2359304 | tf_op jit(solution)/shard_map/ppermute | solution.py:404
  25.5 0.7 copy-start.1
  26.1 33.1 %collective-permute-start.1 = (f32[192,128]{1,0:T(8,128)}, f32[192,128]{1,0:T(8,128)S(1)}, u32[]{:S(2)}, u32[]{:S(2)}) collective-permute-start(f32[192,128]{1,0:T(8,128)} %get-tuple-element.81), channel_id=1, source_target_pairs={{0,16},{16,32},{32,48},{48,64},{64,80},{80,96},{96,112},{112,0},{1... | collective-permute-start | bytes 294920 | tf_op jit(solution)/shard_map/ppermute | solution.py:409
  28.0 35.2 %collective-permute-start.2 = (f32[192,128]{1,0:T(8,128)}, f32[192,128]{1,0:T(8,128)S(1)}, u32[]{:S(2)}, u32[]{:S(2)}) collective-permute-start(f32[192,128]{1,0:T(8,128)} %get-tuple-element.82), channel_id=1, source_target_pairs={{0,32},{16,48},{32,64},{48,80},{64,96},{80,112},{96,0},{112,16},{1... | collective-permute-start | bytes 294920 | tf_op jit(solution)/shard_map/ppermute | solution.py:409
  37.3 35.1 %collective-permute-start.3 = (f32[192,128]{1,0:T(8,128)}, f32[192,128]{1,0:T(8,128)S(1)}, u32[]{:S(2)}, u32[]{:S(2)}) collective-permute-start(f32[192,128]{1,0:T(8,128)} %copy-done.1), channel_id=1, source_target_pairs={{0,48},{16,64},{32,80},{48,96},{64,112},{80,0},{96,16},{112,32},{1... | collective-permute-start | bytes 294920 | tf_op jit(solution)/shard_map/ppermute | solution.py:409
  41.5 34.7 %collective-permute-start.4 = (f32[192,128]{1,0:T(8,128)S(1)}, f32[192,128]{1,0:T(8,128)S(1)}, u32[]{:S(2)}, u32[]{:S(2)}) collective-permute-start(f32[192,128]{1,0:T(8,128)S(1)} %get-tuple-element.84), channel_id=1, source_target_pairs={{0,64},{16,80},{32,96},{48,112},{64,0},{80,16},{96,32},{112,48},{1... | collective-permute-start | bytes 294920 | tf_op jit(solution)/shard_map/ppermute | solution.py:409
  43.9 32.3 %collective-permute-start.5 = (f32[192,128]{1,0:T(8,128)S(1)}, f32[192,128]{1,0:T(8,128)S(1)}, u32[]{:S(2)}, u32[]{:S(2)}) collective-permute-start(f32[192,128]{1,0:T(8,128)S(1)} %get-tuple-element.85), channel_id=1, source_target_pairs={{0,80},{16,96},{32,112},{48,0},{64,16},{80,32},{96,48},{112,64},{1... | collective-permute-start | bytes 294920 | tf_op jit(solution)/shard_map/ppermute | solution.py:409
  59.3 16.9 %collective-permute-start.6 = (f32[192,128]{1,0:T(8,128)S(1)}, f32[192,128]{1,0:T(8,128)S(1)}, u32[]{:S(2)}, u32[]{:S(2)}) collective-permute-start(f32[192,128]{1,0:T(8,128)S(1)} %get-tuple-element.86), channel_id=1, source_target_pairs={{0,96},{16,112},{32,0},{48,16},{64,32},{80,48},{96,64},{112,80},{1... | collective-permute-start | bytes 294920 | tf_op jit(solution)/shard_map/ppermute | solution.py:409
  63.3 13.0 %collective-permute-start.7 = (f32[192,128]{1,0:T(8,128)S(1)}, f32[192,128]{1,0:T(8,128)S(1)}, u32[]{:S(2)}, u32[]{:S(2)}) collective-permute-start(f32[192,128]{1,0:T(8,128)S(1)} %get-tuple-element.87), channel_id=1, source_target_pairs={{0,112},{16,0},{32,16},{48,32},{64,48},{80,64},{96,80},{112,96},{1... | collective-permute-start | bytes 294920 | tf_op jit(solution)/shard_map/ppermute | solution.py:409
  65.5 10.7 %copy-start.2 = (f32[192,128]{1,0:T(8,128)S(1)}, f32[192,128]{1,0:T(8,128)}, u32[]{:S(2)}) copy-start(f32[192,128]{1,0:T(8,128)} %get-tuple-element.80) | copy-start | bytes 294916
  65.5 10.7 %copy-start.5 = (f32[192,3840]{1,0:T(8,128)S(1)}, f32[192,3840]{1,0:T(8,128)}, u32[]{:S(2)}) copy-start(f32[192,3840]{1,0:T(8,128)} %slab_in.3) | copy-start | bytes 8847364
  65.5 10.8 %copy-start.7 = (s32[2,128,128]{2,1,0:T(8,128)S(1)}, s32[2,128,128]{2,1,0:T(8,128)}, u32[]{:S(2)}) copy-start(s32[2,128,128]{2,1,0:T(8,128)} %param.12) | copy-start | bytes 393220
  78.7 24.9 %copy-start = (f32[1,192,1024]{2,1,0:T(8,128)S(1)}, f32[1,192,1024]{2,1,0:T(8,128)}, u32[]{:S(2)}) copy-start(f32[1,192,1024]{2,1,0:T(8,128)} %param.10) | copy-start | bytes 2359300
  78.8 9.3 %collective-permute-start.14 = (f32[192,128]{1,0:T(8,128)S(1)}, f32[192,128]{1,0:T(8,128)S(1)}, u32[]{:S(2)}, u32[]{:S(2)}) collective-permute-start(f32[192,128]{1,0:T(8,128)S(1)} %get-tuple-element.107), channel_id=1, source_target_pairs={{0,112},{16,0},{32,16},{48,32},{64,48},{80,64},{96,80},{112,96},{1... | collective-permute-start | bytes 294920 | tf_op jit(solution)/shard_map/ppermute | solution.py:431
  79.4 10.6 %collective-permute-start.13 = (f32[192,128]{1,0:T(8,128)S(1)}, f32[192,128]{1,0:T(8,128)S(1)}, u32[]{:S(2)}, u32[]{:S(2)}) collective-permute-start(f32[192,128]{1,0:T(8,128)S(1)} %get-tuple-element.108), channel_id=1, source_target_pairs={{0,96},{16,112},{32,0},{48,16},{64,32},{80,48},{96,64},{112,80},{1... | collective-permute-start | bytes 294920 | tf_op jit(solution)/shard_map/ppermute | solution.py:431
  79.4 13.2 %collective-permute-start.12 = (f32[192,128]{1,0:T(8,128)S(1)}, f32[192,128]{1,0:T(8,128)S(1)}, u32[]{:S(2)}, u32[]{:S(2)}) collective-permute-start(f32[192,128]{1,0:T(8,128)S(1)} %get-tuple-element.109), channel_id=1, source_target_pairs={{0,80},{16,96},{32,112},{48,0},{64,16},{80,32},{96,48},{112,64},{1... | collective-permute-start | bytes 294920 | tf_op jit(solution)/shard_map/ppermute | solution.py:431
  82.6 12.5 %collective-permute-start.11 = (f32[192,128]{1,0:T(8,128)S(1)}, f32[192,128]{1,0:T(8,128)S(1)}, u32[]{:S(2)}, u32[]{:S(2)}) collective-permute-start(f32[192,128]{1,0:T(8,128)S(1)} %get-tuple-element.110), channel_id=1, source_target_pairs={{0,64},{16,80},{32,96},{48,112},{64,0},{80,16},{96,32},{112,48},{1... | collective-permute-start | bytes 294920 | tf_op jit(solution)/shard_map/ppermute | solution.py:431
  85.6 13.2 %collective-permute-start.10 = (f32[192,128]{1,0:T(8,128)S(1)}, f32[192,128]{1,0:T(8,128)S(1)}, u32[]{:S(2)}, u32[]{:S(2)}) collective-permute-start(f32[192,128]{1,0:T(8,128)S(1)} %get-tuple-element.111), channel_id=1, source_target_pairs={{0,48},{16,64},{32,80},{48,96},{64,112},{80,0},{96,16},{112,32},{1... | collective-permute-start | bytes 294920 | tf_op jit(solution)/shard_map/ppermute | solution.py:431
  88.2 14.4 %collective-permute-start.9 = (f32[192,128]{1,0:T(8,128)S(1)}, f32[192,128]{1,0:T(8,128)S(1)}, u32[]{:S(2)}, u32[]{:S(2)}) collective-permute-start(f32[192,128]{1,0:T(8,128)S(1)} %get-tuple-element.112), channel_id=1, source_target_pairs={{0,32},{16,48},{32,64},{48,80},{64,96},{80,112},{96,0},{112,16},{1... | collective-permute-start | bytes 294920 | tf_op jit(solution)/shard_map/ppermute | solution.py:431
  90.0 13.7 %collective-permute-start.8 = (f32[192,128]{1,0:T(8,128)S(1)}, f32[192,128]{1,0:T(8,128)S(1)}, u32[]{:S(2)}, u32[]{:S(2)}) collective-permute-start(f32[192,128]{1,0:T(8,128)S(1)} %get-tuple-element.113), channel_id=1, source_target_pairs={{0,16},{16,32},{32,48},{48,64},{64,80},{80,96},{96,112},{112,0},{1... | collective-permute-start | bytes 294920 | tf_op jit(solution)/shard_map/ppermute | solution.py:431
  103.6 17.2 %copy-start.3 = (f32[1,64,128]{2,1,0:T(8,128)S(1)}, f32[1,64,128]{2,1,0:T(8,128)}, u32[]{:S(2)}) copy-start(f32[1,64,128]{2,1,0:T(8,128)} %param.11) | copy-start | bytes 98308
